TPU v7x, 32 devices: a whole 2x2x4 slice. The times are simulated.
32 devices in a mesh: copies: 2 (over x), expert: 4 (over y, core), tm: 4 (over z).
Axes of the slice: x: 2, y: 2, z: 4, core: 2. Of those that a mesh axis runs over, the one named last changes fastest.
Arguments:
- tokens: bfloat16 [4, 1024, 2048], P('tm', ('copies', 'expert')), parts along dimension 1, may hold values from -6 to 6
- route_ids: int32 [4, 1024, 6], P('tm', ('copies', 'expert')), parts along dimension 1, may hold values from 0 to 15, all different within a row; in each aligned block of 128 rows (0 to 127, 128 to 255, ..., all dimensions but the last counted through in order) at most 72 rows name the same one
- route_probs: float32 [4, 1024, 6], P('tm', ('copies', 'expert')), parts along dimension 1, may hold values from 0.05 to 1
- step_size: float32 [8], P(('copies', 'tm')), parts along dimension 0, may hold values from 0.2 to 0.6
- start_state: float32 [1024, 2048], P(('copies', 'expert')), parts along dimension 0, may hold values from -6 to 6
- w_gate: bfloat16 [16, 2048, 768], P('expert'), may hold values from -0.125 to 0.125
- w_up: bfloat16 [16, 2048, 768], P('expert'), may hold values from -0.125 to 0.125
- w_down: bfloat16 [16, 768, 2048], P('expert'), may hold values from -0.21875 to 0.21875
Outputs:
- new_iterate: float32 [4, 1024, 2048], P('tm', ('copies', 'expert')), parts along dimension 1
There are 2 independent parts, one for each index of `copies`. A program takes and returns all parts, laid end to end along the dimension named above; an argument that names none is the same for every part. Nothing has to cross between parts.
Inputs may be any that keep to these rules, and one draw needn't show every extreme that they name: `route_ids`: each row names 6 different experts. In each aligned block of 128 rows (the tokens of one device), no expert is named by more than 72 rows, a bound that some block reaches.
All inputs are finite; a program needn't handle non-finite values.
Results may differ from a plain program's by a relative error of at most 0.0018.
Values may be sent and summed in bfloat16 or wider, within the bound.
No kernel may reach another device: no remote copies, remote signals or barrier semaphores. Data moves between devices by JAX's collectives and lax.ppermute only.
A program may use at most 128 MiB of HBM per device.

v0:
```python
import functools

import jax
import jax.numpy as jnp
from jax import lax
from jax.experimental import pallas as pl
from jax.experimental.pallas import tpu as pltpu
from jax.sharding import PartitionSpec as P

ANY = pl.BlockSpec(memory_space=pl.ANY)
HBM = pl.BlockSpec(memory_space=pltpu.HBM)
VMEM = pl.BlockSpec(memory_space=pltpu.VMEM)
GRANT = pltpu.CompilerParams(vmem_limit_bytes=7 * 1024 * 1024)
BRIEF = pl.CostEstimate(flops=0, bytes_accessed=0, transcendentals=0)
SMALL = pltpu.CompilerParams(vmem_limit_bytes=2 * 1024 * 1024)


def in_hbm(value):
    return pltpu.with_memory_space_constraint(value, pltpu.HBM)


def slots_of(capacity, blocks):
    return -(-capacity * blocks // 16) * 16


def table_kernel(experts, ids_hbm, probs_hbm, tokens_hbm, table, tokens, ids, probs, sems):
    copy = pltpu.make_async_copy(tokens_hbm.at[0], tokens, sems.at[0])
    smalls = [
        pltpu.make_async_copy(ids_hbm, ids, sems.at[1]),
        pltpu.make_async_copy(probs_hbm, probs, sems.at[2]),
    ]
    copy.start()
    for small in smalls:
        small.start()
    for small in smalls:
        small.wait()
    choices, _, count = ids.shape
    total = probs[0]
    for k in range(1, choices):
        total = total + probs[k]
    names = lax.broadcasted_iota(jnp.int32, table.shape, 0)
    value = jnp.zeros(table.shape, jnp.float32)
    for k in range(choices):
        value = value + jnp.where(ids[k] == names, probs[k] / total, 0.0)
    copy.wait()
    rows = tokens[...].astype(jnp.float32)
    scale = lax.rsqrt(jnp.mean(rows * rows, axis=1, keepdims=True) + 1e-06)
    scale = jnp.broadcast_to(scale, (count, 128)).T[:1]
    table[...] = jnp.where(names == experts, scale, value)


def make_table(ids, probs, tokens, experts):
    count, features = tokens.shape[1:]
    height = -(-(experts + 1) // 8) * 8
    ids, probs = jnp.transpose(ids, (2, 0, 1)), jnp.transpose(probs, (2, 0, 1))
    return pl.pallas_call(
        functools.partial(table_kernel, experts),
        out_shape=(
            pltpu.VMEM((height, count), jnp.float32),
            pltpu.VMEM((count, features), tokens.dtype),
        ),
        in_specs=[HBM] * 3,
        out_specs=(VMEM, VMEM),
        scratch_shapes=[
            pltpu.VMEM(ids.shape, ids.dtype),
            pltpu.VMEM(probs.shape, probs.dtype),
            pltpu.SemaphoreType.DMA((3,)),
        ],
        compiler_params=SMALL,
        name="make_table",
    )(in_hbm(ids), in_hbm(probs), in_hbm(tokens))


def plan(tables, capacity, hots, coefs):
    local, slots, width = hots.shape
    blocks = len(tables)
    count = width // blocks
    experts = local * lax.axis_size("expert")
    first = lax.axis_index("expert") * local
    before = lax.broadcasted_iota(jnp.int32, (count, count), 0)
    after = lax.broadcasted_iota(jnp.int32, (count, count), 1)
    upto = jnp.where(before <= after, 1.0, 0.0).astype(jnp.bfloat16)
    slot_ids = lax.broadcasted_iota(jnp.int32, (slots, width), 0).astype(jnp.float32)
    weights, scales, places = [], [], []
    for b in range(blocks):
        weight = tables[b][pl.ds(first, local), :]
        ones = jnp.where(weight > 0.0, 1.0, 0.0)
        padded = jnp.concatenate([ones, jnp.zeros((-local % 16, count), jnp.float32)], axis=0)
        rank = jnp.dot(padded.astype(jnp.bfloat16), upto, preferred_element_type=jnp.float32)[:local]
        places.append(jnp.where(weight > 0.0, rank + float(b * capacity - 1), -1.0))
        weights.append(weight)
        scales.append(tables[b][pl.ds(experts, 1), :])
    weight = jnp.concatenate(weights, axis=1) if blocks > 1 else weights[0]
    scale = jnp.concatenate(scales, axis=1) if blocks > 1 else scales[0]
    place = jnp.concatenate(places, axis=1) if blocks > 1 else places[0]
    for j in range(local):
        hit = slot_ids == place[j : j + 1, :]
        hots[j] = jnp.where(hit, 1.0, 0.0).astype(jnp.bfloat16)
        coefs[j, :, 0:1] = jnp.sum(jnp.where(hit, scale, 0.0), axis=1, keepdims=True)
        coefs[j, :, 1:2] = jnp.sum(jnp.where(hit, weight[j : j + 1, :], 0.0), axis=1, keepdims=True)


def pack(hots, tokens, rows):
    for j in range(hots.shape[0]):
        rows[j] = jnp.dot(hots[j], tokens, preferred_element_type=jnp.float32).astype(jnp.bfloat16)


def expert_hidden(j, rows, hots, coefs, gates, ups, out_ref, base):
    units = gates.shape[2]
    size = hots.shape[2]
    gate = jnp.dot(rows[j], gates[j], preferred_element_type=jnp.float32)
    up = jnp.dot(rows[j], ups[j], preferred_element_type=jnp.float32)
    scale = coefs[j, :, 0:1]
    weight = coefs[j, :, 1:2]
    g = gate * scale
    h = (g / (1.0 + jnp.exp(-g))) * (up * (scale * weight))
    placed = lax.dot_general(
        hots[j], h.astype(jnp.bfloat16), (((0,), (0,)), ((), ())), preferred_element_type=jnp.float32
    )
    out_ref[pl.ds(base, size), pl.ds(j * units, units)] = placed.astype(jnp.bfloat16)


def near_kernel(capacity, *refs):
    tables, tokens = refs[:2], refs[2:4]
    gate_hbm, up_hbm, hidden, gates, ups = refs[4:9]
    hots, coefs, rows, gate_sem, up_sem = refs[9:]
    local = gates.shape[0]
    copies = []
    for j in range(local):
        copies.append(pltpu.make_async_copy(gate_hbm.at[j], gates.at[j], gate_sem.at[j]))
        copies.append(pltpu.make_async_copy(up_hbm.at[j], ups.at[j], up_sem.at[j]))
    for copy in copies:
        copy.start()
    plan(tables, capacity, hots, coefs)
    pack(hots, jnp.concatenate([t[...] for t in tokens], axis=0), rows)
    for j in range(local):
        copies[2 * j].wait()
        copies[2 * j + 1].wait()
        expert_hidden(j, rows, hots, coefs, gates, ups, hidden, 0)


def near_hidden(tables, tokens, w_gate, w_up, capacity, blocks):
    count, features = tokens[0].shape
    local, _, units = w_gate.shape
    slots = slots_of(capacity, 2)
    return pl.pallas_call(
        functools.partial(near_kernel, capacity),
        out_shape=(
            pltpu.VMEM((blocks * count, local * units), jnp.bfloat16),
            pltpu.VMEM(w_gate.shape, w_gate.dtype),
            pltpu.VMEM(w_up.shape, w_up.dtype),
        ),
        in_specs=[VMEM] * 4 + [HBM] * 2,
        out_specs=(VMEM,) * 3,
        scratch_shapes=[
            pltpu.VMEM((local, slots, 2 * count), jnp.bfloat16),
            pltpu.VMEM((local, slots, 128), jnp.float32),
            pltpu.VMEM((local, slots, features), jnp.bfloat16),
            pltpu.SemaphoreType.DMA((local,)),
            pltpu.SemaphoreType.DMA((local,)),
        ],
        compiler_params=GRANT,
        cost_estimate=pl.CostEstimate(
            flops=4 * local * slots * features * units,
            bytes_accessed=4 * local * features * units,
            transcendentals=local * slots * units,
        ),
        name="near_hidden",
    )(*tables, *tokens, in_hbm(w_gate), in_hbm(w_up))


def far_plan_kernel(capacity, far_count, *refs):
    tables = refs[:far_count]
    step, _, hots, coefs, factor = refs[far_count:]
    factor[...] = jnp.full(factor.shape, step[0])
    for p in range(far_count // 2):
        plan(tables[2 * p : 2 * p + 2], capacity, hots.at[p], coefs.at[p])


def far_plan(tables, step_size, order, capacity, local):
    pairs = len(tables) // 2
    count = tables[0].shape[1]
    slots = slots_of(capacity, 2)
    return pl.pallas_call(
        functools.partial(far_plan_kernel, capacity, len(tables)),
        out_shape=(
            pltpu.VMEM((pairs, local, slots, 2 * count), jnp.bfloat16),
            pltpu.VMEM((pairs, local, slots, 128), jnp.float32),
            pltpu.VMEM((8, 128), jnp.float32),
        ),
        in_specs=[VMEM] * len(tables) + [pl.BlockSpec(memory_space=pltpu.SMEM), ANY],
        out_specs=(VMEM,) * 3,
        compiler_params=SMALL,
        cost_estimate=BRIEF,
        name="far_plan",
    )(*tables, step_size, order)


def far_kernel(far_count, *refs):
    tokens = refs[:far_count]
    hots, coefs, gates, ups, down_hbm, start_hbm, _, hidden, downs, start, rows, sems = refs[far_count:]
    copies = [
        pltpu.make_async_copy(down_hbm, downs, sems.at[0]),
        pltpu.make_async_copy(start_hbm, start, sems.at[1]),
    ]
    for copy in copies:
        copy.start()
    for p in range(far_count // 2):
        both = jnp.concatenate([tokens[2 * p][...], tokens[2 * p + 1][...]], axis=0)
        pack(hots.at[p], both, rows)
        for j in range(gates.shape[0]):
            expert_hidden(j, rows, hots.at[p], coefs.at[p], gates, ups, hidden, (p + 1) * hots.shape[3])
    for copy in copies:
        copy.wait()


def far_hidden(tokens, hots, coefs, gates, ups, w_down, start_state, hidden):
    pairs, local, slots, size = hots.shape
    features, units = gates.shape[1:]
    return pl.pallas_call(
        functools.partial(far_kernel, len(tokens)),
        out_shape=(
            pltpu.VMEM(hidden.shape, hidden.dtype),
            pltpu.VMEM(w_down.shape, w_down.dtype),
            pltpu.VMEM(start_state.shape, start_state.dtype),
        ),
        in_specs=[VMEM] * (len(tokens) + 4) + [HBM] * 2 + [VMEM],
        out_specs=(VMEM,) * 3,
        scratch_shapes=[
            pltpu.VMEM((local, slots, features), jnp.bfloat16),
            pltpu.SemaphoreType.DMA((2,)),
        ],
        input_output_aliases={len(tokens) + 6: 0},
        compiler_params=GRANT,
        cost_estimate=pl.CostEstimate(
            flops=4 * pairs * local * slots * features * units,
            bytes_accessed=6 * local * features * units,
            transcendentals=pairs * local * slots * units,
        ),
        name="far_hidden",
    )(*tokens, hots, coefs, gates, ups, in_hbm(w_down), in_hbm(start_state), hidden)


def down_kernel(core, start, hidden_ref, down_ref, _, out_ref):
    pairs, count, width = out_ref.shape
    local, units, _ = down_ref.shape
    columns = pl.ds(start, width)
    total = None
    for j in range(local):
        inner = pl.ds(j * units, units)
        parts = [hidden_ref[pl.ds((2 * p + core) * count, count), inner] for p in range(pairs)]
        term = jnp.dot(
            jnp.concatenate(parts, axis=0), down_ref[j, :, columns], preferred_element_type=jnp.float32
        )
        total = term if total is None else total + term
    for p in range(pairs):
        out_ref[p] = total[p * count : (p + 1) * count].astype(out_ref.dtype)


def down_rows(hidden, downs, order, send, count, start, width):
    pairs = hidden.shape[0] // (2 * count)
    return pl.pallas_call(
        functools.partial(down_kernel, int(send), start),
        out_shape=pltpu.VMEM((pairs, count, width), jnp.bfloat16 if send else jnp.float32),
        in_specs=[VMEM, VMEM, ANY],
        out_specs=VMEM,
        compiler_params=GRANT,
        cost_estimate=BRIEF,
        name="down_rows",
    )(hidden, downs, order)


def core_sum_kernel(chunks, keep, got, factor, _, *outs):
    pairs, _, width = keep.shape
    width = width // chunks
    step = factor[0:1, 0:1]
    for i in range(chunks):
        columns = pl.ds(i * width, width)
        for p in range(pairs):
            total = step * (keep[p, :, columns] + got[p, :, columns].astype(jnp.float32))
            if p == 0:
                outs[2 * i][...] = total
            else:
                outs[2 * i + 1][p - 1] = total.astype(jnp.bfloat16)


def core_sum(keep, got, factor, order, chunks):
    pairs, count, width = keep.shape
    shapes = []
    for _ in range(chunks):
        shapes.append(pltpu.VMEM((count, width // chunks), jnp.float32))
        shapes.append(pltpu.VMEM((pairs - 1, count, width // chunks), jnp.bfloat16))
    return pl.pallas_call(
        functools.partial(core_sum_kernel, chunks),
        out_shape=tuple(shapes),
        in_specs=[VMEM, VMEM, VMEM, ANY],
        out_specs=(VMEM,) * len(shapes),
        compiler_params=SMALL,
        cost_estimate=BRIEF,
        name="core_sum",
    )(keep, got, factor, order)


def chain_kernel(hop, backs, first, send, start, _, own, *refs):
    outs = refs[len(refs) - 1 - send :]
    result, width = outs[-1], own.shape[1]

    @pl.when(lax.axis_index("tm") == hop)
    def _():
        total = own[...]
        for ref in refs[: backs + (hop > 0)]:
            total = total + ref[...].astype(jnp.float32)
        if send:
            outs[0][...] = total.astype(jnp.bfloat16)
        columns = pl.ds(first, width)
        result[:, columns] = start[:, columns] + total


def chain_step(hop, own, backs, got, first, send, start, result, order):
    inputs = [start, order, own, *backs] + ([] if got is None else [got]) + ([] if result is None else [result])
    return pl.pallas_call(
        functools.partial(chain_kernel, hop, len(backs), first, int(send)),
        out_shape=((pltpu.VMEM(own.shape, jnp.bfloat16),) if send else ())
        + (pltpu.VMEM(start.shape, jnp.float32),),
        in_specs=[VMEM, ANY] + [VMEM] * (len(inputs) - 2),
        out_specs=(VMEM,) * (1 + send),
        input_output_aliases={} if result is None else {len(inputs) - 1: int(send)},
        compiler_params=SMALL,
        cost_estimate=BRIEF,
        name="chain_step",
    )(*inputs)


def write_kernel(result, out, sem):
    copy = pltpu.make_async_copy(result, out, sem)
    copy.start()
    copy.wait()


def write_out(result):
    return pl.pallas_call(
        write_kernel,
        out_shape=pltpu.HBM(result.shape, result.dtype),
        in_specs=[VMEM],
        out_specs=HBM,
        scratch_shapes=[pltpu.SemaphoreType.DMA],
        compiler_params=SMALL,
        cost_estimate=BRIEF,
        name="write_out",
    )(result)


def tie_kernel(value_ref, order_ref, out_ref):
    pass


def tie(value, order):
    return pl.pallas_call(
        tie_kernel,
        out_shape=jax.ShapeDtypeStruct(value.shape, value.dtype),
        in_specs=[ANY, ANY],
        out_specs=ANY,
        input_output_aliases={0: 0},
        compiler_params=SMALL,
        cost_estimate=BRIEF,
        name="tie",
    )(value, order)


def exchange(value, low, members, steps):
    pairs = []
    for e in range(members):
        for z in range(steps):
            if z in (low, low + 1):
                pairs.append((e * steps + z, e * steps + 2 * low + 1 - z))
            else:
                pairs.append((e * steps + z, (e ^ 1) * steps + z))
    return lax.ppermute(value, ("expert", "tm"), pairs)


def shards(tokens, route_ids, route_probs, step_size, start_state, w_gate, w_up, w_down):
    members = lax.axis_size("expert")
    steps = lax.axis_size("tm")
    tok_count, feature_count = tokens.shape[1:]
    topk_count = route_ids.shape[2]
    expert_total = w_gate.shape[0] * members
    capacity = 3 * tok_count * topk_count // (2 * expert_total)
    chips = members // 2

    def swapped(value):
        return lax.ppermute(value, "expert", [(i, i ^ 1) for i in range(members)])

    def shifted(value, by):
        return lax.ppermute(value, "expert", [(i, (i + 2 * by) % members) for i in range(members)])

    own = tokens[0]
    far_same = [shifted(own, by) for by in range(1, chips)]
    partner = swapped(own)
    table, own = make_table(route_ids, route_probs, tokens, expert_total)
    far_table = [shifted(table, by) for by in range(1, chips)]
    hidden, gates, ups = near_hidden([table, swapped(table)], [own, partner], w_gate, w_up, capacity, members)
    far_tables, far_tokens = [], []
    for value, piece in zip(far_table, far_same):
        value = tie(value, hidden)
        piece = tie(piece, value)
        far_tables += [value, swapped(value)]
        far_tokens += [piece, swapped(piece)]
    hots, coefs, factor = far_plan(far_tables, step_size, hidden, capacity, w_gate.shape[0])
    hidden, downs, start = far_hidden(far_tokens, hots, coefs, gates, ups, w_down, start_state, hidden)

    parts = 4
    width = feature_count // parts
    groups = [(0, 1), (1, parts - 1)]
    events, ready = [], 0.0
    for g, (_, count) in enumerate(groups):
        events.append((ready, "send", g, 0))
        events.append((ready + 0.9 * count, "keep", g, 0))
        ready += max(2.5, 1.8 * count)
        events.append((ready, "core", g, 0))
    for c in range(parts):
        for hop in range(steps):
            events.append((12.0 + 3.3 * c + 5.0 * hop, "chain", c, hop))
    order, result = hidden, None
    gots, keeps, owns, backs, arrived = {}, {}, {}, {}, {}
    for _, kind, c, hop in sorted(events):
        if kind in ("send", "keep"):
            first, count = groups[c]
            part = down_rows(hidden, downs, order, kind == "send", tok_count, first * width, count * width)
            if kind == "send":
                gots[c] = swapped(part)
            else:
                keeps[c] = part
            order = part
        elif kind == "core":
            first, count = groups[c]
            sums = core_sum(keeps[c], gots[c], factor, order, count)
            for i in range(count):
                owns[first + i] = sums[2 * i]
                backs[first + i] = [shifted(sums[2 * i + 1][by - 1], -by) for by in range(1, chips)]
            order = sums[0]
        else:
            send = hop < steps - 1
            *sent, result = chain_step(
                hop, owns[c], backs[c], arrived.get(c), c * width, send, start, result, order
            )
            if send:
                order = sent[0]
                arrived[c] = exchange(sent[0], hop, members, steps)
    return write_out(result)[None]


def solution(mesh):
    return jax.shard_map(
        shards,
        mesh=mesh,
        in_specs=(
            P("tm", ("copies", "expert"), None),
            P("tm", ("copies", "expert"), None),
            P("tm", ("copies", "expert"), None),
            P(("copies", "tm")),
            P(("copies", "expert"), None),
            P("expert", None, None),
            P("expert", None, None),
            P("expert", None, None),
        ),
        out_specs=P("tm", ("copies", "expert"), None),
        check_vma=False,
    )
```

profile of v0, /device:TPU:16, one launch (start us, length us, event | category | flops | bytes accessed | tf_op | source)
XLA Modules:
  0.0 61.6 jit_solution(12290650131273120833)
XLA Ops:
  0.0 1.5 %collective-permute-start = (bf16[128,2048]{1,0:T(8,128)(2,1)}, bf16[128,2048]{1,0:T(8,128)(2,1)S(1)}, u32[]{:S(2)}, u32[]{:S(2)}) collective-permute-start(bf16[128,2048]{1,0:T(8,128)(2,1)} %bitcast.13), channel_id=1, source_target_pairs={{0,8},{4,12},{8,0},{12,4},{1,9},{5,13},{9,1},{13,5},{2,10},{6,14},... | collective-permute-start | bytes 1572872 | tf_op jit(solution)/shard_map/ppermute | solution.py:394
  1.5 1.3 %make_table.1 = (f32[24,128]{1,0:T(8,128)S(1)}, bf16[128,2048]{1,0:T(8,128)(2,1)S(1)}) custom-call(s32[6,1,128]{2,1,0:T(1,128)} %bitcast.14, f32[6,1,128]{2,1,0:T(1,128)} %bitcast.15, bf16[1,128,2048]{2,1,0:T(8,128)(2,1)} %tokens_hbm.1), custom_call_target="tpu_custom_call" | custom-call | tf_op jit(solution)/shard_map/make_table/pallas_call | solution.py:56
  2.9 0.3 collective-permute-start.2
  3.2 0.5 collective-permute-start.1
  3.7 0.4 collective-permute-done.2.refs_1_
  4.1 10.2 %near_hidden.1 = (bf16[512,3072]{1,0:T(8,128)(2,1)S(1)}, bf16[4,2048,768]{2,1,0:T(8,128)(2,1)S(1)}, bf16[4,2048,768]{2,1,0:T(8,128)(2,1)S(1)}) custom-call(f32[24,128]{1,0:T(8,128)S(1)} %get-tuple-element.48.refs_0_, f32[24,128]{1,0:T(8,128)S(1)} %collective-permute-done.2.refs_1_, bf16[128,2048]{1,0:T(8,128)(2,1)S(1)} %get-tuple-element.49.refs_2_, ...), custom_call_target="tpu_custom_call" | custom-call | flops 3623878656 | bytes 25165824 | tf_op jit(solution)/shard_map/near_hidden/pallas_call | solution.py:146
  14.3 0.5 collective-permute-done.1.value_ref
  14.8 0.0 collective-permute-start.4
  14.8 0.5 collective-permute-start.5
  16.0 0.8 %collective-permute-done.5.refs_1_ = f32[24,128]{1,0:T(8,128)S(1)} collective-permute-done((f32[24,128]{1,0:T(8,128)S(1)}, f32[24,128]{1,0:T(8,128)S(1)}, u32[]{:S(2)}, u32[]{:S(2)}) %collective-permute-start.5) | collective-permute-done | bytes 12320 | tf_op jit(solution)/shard_map/ppermute | solution.py:391
  16.7 0.4 far_plan.1
  17.1 5.4 %far_hidden.1 = (bf16[512,3072]{1,0:T(8,128)(2,1)S(1)}, bf16[4,768,2048]{2,1,0:T(8,128)(2,1)S(1)}, f32[128,2048]{1,0:T(8,128)S(1)}) custom-call(bf16[128,2048]{1,0:T(8,128)(2,1)S(1)} %tie.3.refs_0_, bf16[128,2048]{1,0:T(8,128)(2,1)S(1)} %collective-permute-done.4.refs_1_, ...), custom_call_target="tpu_custom_call", output_to_operand_aliasing={{0}: (8, {})} | custom-call | flops 3623878656 | bytes 37748736 | tf_op jit(solution)/shard_map/far_hidden/pallas_call | solution.py:220
  22.6 1.2 %down_rows.4._ = bf16[2,128,512]{2,1,0:T(8,128)(2,1)S(1)} custom-call(bf16[512,3072]{1,0:T(8,128)(2,1)S(1)} %get-tuple-element.56.hidden_ref._, bf16[4,768,2048]{2,1,0:T(8,128)(2,1)S(1)} %get-tuple-element.57.down_ref, bf16[512,3072]{1,0:T(8,128)(2,1)S(1)} %get-tuple-element.56.hidden_ref._), custom_call_target="tpu_custom_call" | custom-call | tf_op jit(solution)/shard_map/down_rows/pallas_call | solution.py:262
  23.7 0.2 collective-permute-start.6
  23.9 1.0 %down_rows.5.keep._ = f32[2,128,512]{2,1,0:T(8,128)S(1)} custom-call(bf16[512,3072]{1,0:T(8,128)(2,1)S(1)} %get-tuple-element.56.hidden_ref._, bf16[4,768,2048]{2,1,0:T(8,128)(2,1)S(1)} %get-tuple-element.57.down_ref, bf16[2,128,512]{2,1,0:T(8,128)(2,1)S(1)} %down_rows.4._), custom_call_target="tpu_custom_call" | custom-call | tf_op jit(solution)/shard_map/down_rows/pallas_call | solution.py:262
  24.9 0.4 collective-permute-done.6.got
  25.3 0.1 core_sum.2
  25.4 2.6 %down_rows.6._ = bf16[2,128,1536]{2,1,0:T(8,128)(2,1)S(1)} custom-call(bf16[512,3072]{1,0:T(8,128)(2,1)S(1)} %get-tuple-element.56.hidden_ref._, bf16[4,768,2048]{2,1,0:T(8,128)(2,1)S(1)} %get-tuple-element.57.down_ref, f32[128,512]{1,0:T(8,128)S(1)} %get-tuple-element.59._.own), custom_call_target="tpu_custom_call" | custom-call | tf_op jit(solution)/shard_map/down_rows/pallas_call | solution.py:262
  28.0 0.2 collective-permute-start.7
  28.2 1.5 %collective-permute-start.8 = (bf16[128,512]{1,0:T(8,128)(2,1)S(1)}, bf16[128,512]{1,0:T(8,128)(2,1)S(1)}, u32[]{:S(2)}, u32[]{:S(2)}) collective-permute-start(bf16[128,512]{1,0:T(8,128)(2,1)S(1)} %bitcast.10), channel_id=1, source_target_pairs={{0,8},{4,12},{8,0},{12,4},{1,9},{5,13},{9,1},{13,5},{2,10},{6,14},... | collective-permute-start | bytes 393224 | tf_op jit(solution)/shard_map/ppermute | solution.py:394
  29.8 2.6 %down_rows.7.keep._ = f32[2,128,1536]{2,1,0:T(8,128)S(1)} custom-call(bf16[512,3072]{1,0:T(8,128)(2,1)S(1)} %get-tuple-element.56.hidden_ref._, bf16[4,768,2048]{2,1,0:T(8,128)(2,1)S(1)} %get-tuple-element.57.down_ref, bf16[2,128,1536]{2,1,0:T(8,128)(2,1)S(1)} %down_rows.6._), custom_call_target="tpu_custom_call" | custom-call | tf_op jit(solution)/shard_map/down_rows/pallas_call | solution.py:262
  32.4 0.0 collective-permute-done.7.got
  32.4 0.2 core_sum.3
  32.6 0.6 collective-permute-start.9
  33.2 0.8 %collective-permute-done.8.refs_0_ = bf16[128,512]{1,0:T(8,128)(2,1)S(1)} collective-permute-done((bf16[128,512]{1,0:T(8,128)(2,1)S(1)}, bf16[128,512]{1,0:T(8,128)(2,1)S(1)}, u32[]{:S(2)}, u32[]{:S(2)}) %collective-permute-start.8) | collective-permute-done | bytes 131104 | tf_op jit(solution)/shard_map/ppermute | solution.py:394
  34.0 1.5 %collective-permute-start.11 = (bf16[128,512]{1,0:T(8,128)(2,1)S(1)}, bf16[128,512]{1,0:T(8,128)(2,1)S(1)}, u32[]{:S(2)}, u32[]{:S(2)}) collective-permute-start(bf16[128,512]{1,0:T(8,128)(2,1)S(1)} %bitcast.9), channel_id=1, source_target_pairs={{0,8},{4,12},{8,0},{12,4},{1,9},{5,13},{9,1},{13,5},{2,10},{6,14},... | collective-permute-start | bytes 393224 | tf_op jit(solution)/shard_map/ppermute | solution.py:394
  35.5 3.5 %collective-permute-done.9.refs_0_ = bf16[128,512]{1,0:T(8,128)(2,1)S(1)} collective-permute-done((bf16[128,512]{1,0:T(8,128)(2,1)S(1)}, bf16[128,512]{1,0:T(8,128)(2,1)S(1)}, u32[]{:S(2)}, u32[]{:S(2)}) %collective-permute-start.9) | collective-permute-done | bytes 131104 | tf_op jit(solution)/shard_map/ppermute | solution.py:394
  39.1 0.9 %collective-permute-start.14 = (bf16[128,512]{1,0:T(8,128)(2,1)S(1)}, bf16[128,512]{1,0:T(8,128)(2,1)S(1)}, u32[]{:S(2)}, u32[]{:S(2)}) collective-permute-start(bf16[128,512]{1,0:T(8,128)(2,1)S(1)} %get-tuple-element.67._), channel_id=1, source_target_pairs={{0,4},{1,2},{2,1},{3,7},{4,0},{5,6},{6,5},{7,3},{8,12},{9,10},{10,... | collective-permute-start | bytes 393224 | tf_op jit(solution)/shard_map/ppermute | solution.py:378
  40.0 1.0 %collective-permute-done.11.refs_0_ = bf16[128,512]{1,0:T(8,128)(2,1)S(1)} collective-permute-done((bf16[128,512]{1,0:T(8,128)(2,1)S(1)}, bf16[128,512]{1,0:T(8,128)(2,1)S(1)}, u32[]{:S(2)}, u32[]{:S(2)}) %collective-permute-start.11) | collective-permute-done | bytes 131104 | tf_op jit(solution)/shard_map/ppermute | solution.py:394
  41.0 4.2 %collective-permute-start.16 = (bf16[128,512]{1,0:T(8,128)(2,1)S(1)}, bf16[128,512]{1,0:T(8,128)(2,1)S(1)}, u32[]{:S(2)}, u32[]{:S(2)}) collective-permute-start(bf16[128,512]{1,0:T(8,128)(2,1)S(1)} %get-tuple-element.73._), channel_id=1, source_target_pairs={{0,4},{1,2},{2,1},{3,7},{4,0},{5,6},{6,5},{7,3},{8,12},{9,10},{10,... | collective-permute-start | bytes 393224 | tf_op jit(solution)/shard_map/ppermute | solution.py:378
  45.2 0.3 collective-permute-done.14.refs_1_
  45.5 0.1 chain_step.22
  45.5 1.1 %collective-permute-start.19 = (bf16[128,512]{1,0:T(8,128)(2,1)S(1)}, bf16[128,512]{1,0:T(8,128)(2,1)S(1)}, u32[]{:S(2)}, u32[]{:S(2)}) collective-permute-start(bf16[128,512]{1,0:T(8,128)(2,1)S(1)} %get-tuple-element.79._), channel_id=1, source_target_pairs={{0,4},{1,5},{2,3},{3,2},{4,0},{5,1},{6,7},{7,6},{8,12},{9,13},{10,... | collective-permute-start | bytes 393224 | tf_op jit(solution)/shard_map/ppermute | solution.py:378
  46.6 1.8 %collective-permute-start.18 = (bf16[128,512]{1,0:T(8,128)(2,1)S(1)}, bf16[128,512]{1,0:T(8,128)(2,1)S(1)}, u32[]{:S(2)}, u32[]{:S(2)}) collective-permute-start(bf16[128,512]{1,0:T(8,128)(2,1)S(1)} %get-tuple-element.81._), channel_id=1, source_target_pairs={{0,4},{1,2},{2,1},{3,7},{4,0},{5,6},{6,5},{7,3},{8,12},{9,10},{10,... | collective-permute-start | bytes 393224 | tf_op jit(solution)/shard_map/ppermute | solution.py:378
  48.4 0.1 chain_step.24
  48.5 0.1 collective-permute-start.21
  48.6 2.0 %collective-permute-start.20 = (bf16[128,512]{1,0:T(8,128)(2,1)S(1)}, bf16[128,512]{1,0:T(8,128)(2,1)S(1)}, u32[]{:S(2)}, u32[]{:S(2)}) collective-permute-start(bf16[128,512]{1,0:T(8,128)(2,1)S(1)} %get-tuple-element.85._), channel_id=1, source_target_pairs={{0,4},{1,2},{2,1},{3,7},{4,0},{5,6},{6,5},{7,3},{8,12},{9,10},{10,... | collective-permute-start | bytes 393224 | tf_op jit(solution)/shard_map/ppermute | solution.py:378
  50.6 1.3 %collective-permute-done.19.refs_1_ = bf16[128,512]{1,0:T(8,128)(2,1)S(1)} collective-permute-done((bf16[128,512]{1,0:T(8,128)(2,1)S(1)}, bf16[128,512]{1,0:T(8,128)(2,1)S(1)}, u32[]{:S(2)}, u32[]{:S(2)}) %collective-permute-start.19) | collective-permute-done | bytes 131104 | tf_op jit(solution)/shard_map/ppermute | solution.py:378
  51.9 0.5 collective-permute-done.18.refs_1_
  52.4 0.1 chain_step.27
  52.5 0.6 collective-permute-start.23
  53.1 1.0 %collective-permute-done.21.refs_1_ = bf16[128,512]{1,0:T(8,128)(2,1)S(1)} collective-permute-done((bf16[128,512]{1,0:T(8,128)(2,1)S(1)}, bf16[128,512]{1,0:T(8,128)(2,1)S(1)}, u32[]{:S(2)}, u32[]{:S(2)}) %collective-permute-start.21) | collective-permute-done | bytes 131104 | tf_op jit(solution)/shard_map/ppermute | solution.py:378
  54.0 1.0 %collective-permute-done.20.refs_1_ = bf16[128,512]{1,0:T(8,128)(2,1)S(1)} collective-permute-done((bf16[128,512]{1,0:T(8,128)(2,1)S(1)}, bf16[128,512]{1,0:T(8,128)(2,1)S(1)}, u32[]{:S(2)}, u32[]{:S(2)}) %collective-permute-start.20) | collective-permute-done | bytes 131104 | tf_op jit(solution)/shard_map/ppermute | solution.py:378
  55.0 0.1 chain_step.29
  55.1 0.7 %collective-permute-start.22 = (bf16[128,512]{1,0:T(8,128)(2,1)S(1)}, bf16[128,512]{1,0:T(8,128)(2,1)S(1)}, u32[]{:S(2)}, u32[]{:S(2)}) collective-permute-start(bf16[128,512]{1,0:T(8,128)(2,1)S(1)} %get-tuple-element.89._), channel_id=1, source_target_pairs={{0,4},{1,5},{2,3},{3,2},{4,0},{5,1},{6,7},{7,6},{8,12},{9,13},{10,... | collective-permute-start | bytes 393224 | tf_op jit(solution)/shard_map/ppermute | solution.py:378
  55.8 1.7 %collective-permute-done.23.refs_1_ = bf16[128,512]{1,0:T(8,128)(2,1)S(1)} collective-permute-done((bf16[128,512]{1,0:T(8,128)(2,1)S(1)}, bf16[128,512]{1,0:T(8,128)(2,1)S(1)}, u32[]{:S(2)}, u32[]{:S(2)}) %collective-permute-start.23) | collective-permute-done | bytes 131104 | tf_op jit(solution)/shard_map/ppermute | solution.py:378
  57.5 2.9 %collective-permute-done.22.refs_1_ = bf16[128,512]{1,0:T(8,128)(2,1)S(1)} collective-permute-done((bf16[128,512]{1,0:T(8,128)(2,1)S(1)}, bf16[128,512]{1,0:T(8,128)(2,1)S(1)}, u32[]{:S(2)}, u32[]{:S(2)}) %collective-permute-start.22) | collective-permute-done | bytes 131104 | tf_op jit(solution)/shard_map/ppermute | solution.py:378
  60.5 1.0 %write_out.1 = f32[128,2048]{1,0:T(8,128)} custom-call(f32[128,2048]{1,0:T(8,128)S(1)} %chain_step.31.result), custom_call_target="tpu_custom_call" | custom-call | tf_op jit(solution)/shard_map/write_out/pallas_call | solution.py:341
  (29 shorter events, 0.1 us)
Async XLA Ops:
  0.0 4.1 %collective-permute-start.3 = (bf16[128,2048]{1,0:T(8,128)(2,1)}, bf16[128,2048]{1,0:T(8,128)(2,1)S(1)}, u32[]{:S(2)}, u32[]{:S(2)}) collective-permute-start(bf16[128,2048]{1,0:T(8,128)(2,1)} %bitcast.12), channel_id=1, source_target_pairs={{0,4},{4,0},{8,12},{12,8},{1,5},{5,1},{9,13},{13,9},{2,6},{6,2},{1... | collective-permute-start | bytes 1572872 | tf_op jit(solution)/shard_map/ppermute | solution.py:391
  0.0 14.8 %collective-permute-start = (bf16[128,2048]{1,0:T(8,128)(2,1)}, bf16[128,2048]{1,0:T(8,128)(2,1)S(1)}, u32[]{:S(2)}, u32[]{:S(2)}) collective-permute-start(bf16[128,2048]{1,0:T(8,128)(2,1)} %bitcast.13), channel_id=1, source_target_pairs={{0,8},{4,12},{8,0},{12,4},{1,9},{5,13},{9,1},{13,5},{2,10},{6,14},... | collective-permute-start | bytes 1572872 | tf_op jit(solution)/shard_map/ppermute | solution.py:394
  2.9 1.2 %collective-permute-start.2 = (f32[24,128]{1,0:T(8,128)S(1)}, f32[24,128]{1,0:T(8,128)S(1)}, u32[]{:S(2)}, u32[]{:S(2)}) collective-permute-start(f32[24,128]{1,0:T(8,128)S(1)} %get-tuple-element.48.refs_0_), channel_id=1, source_target_pairs={{0,4},{4,0},{8,12},{12,8},{1,5},{5,1},{9,13},{13,9},{2,6},{6,2},{1... | collective-permute-start | bytes 36872 | tf_op jit(solution)/shard_map/ppermute | solution.py:391
  3.2 11.7 %collective-permute-start.1 = (f32[24,128]{1,0:T(8,128)S(1)}, f32[24,128]{1,0:T(8,128)S(1)}, u32[]{:S(2)}, u32[]{:S(2)}) collective-permute-start(f32[24,128]{1,0:T(8,128)S(1)} %get-tuple-element.48.refs_0_), channel_id=1, source_target_pairs={{0,8},{4,12},{8,0},{12,4},{1,9},{5,13},{9,1},{13,5},{2,10},{6,14},... | collective-permute-start | bytes 36872 | tf_op jit(solution)/shard_map/ppermute | solution.py:394
  14.8 2.3 %collective-permute-start.4 = (bf16[128,2048]{1,0:T(8,128)(2,1)S(1)}, bf16[128,2048]{1,0:T(8,128)(2,1)S(1)}, u32[]{:S(2)}, u32[]{:S(2)}) collective-permute-start(bf16[128,2048]{1,0:T(8,128)(2,1)S(1)} %tie.3.refs_0_), channel_id=1, source_target_pairs={{0,4},{4,0},{8,12},{12,8},{1,5},{5,1},{9,13},{13,9},{2,6},{6,2},{1... | collective-permute-start | bytes 1572872 | tf_op jit(solution)/shard_map/ppermute | solution.py:391
  14.8 1.9 %collective-permute-start.5 = (f32[24,128]{1,0:T(8,128)S(1)}, f32[24,128]{1,0:T(8,128)S(1)}, u32[]{:S(2)}, u32[]{:S(2)}) collective-permute-start(f32[24,128]{1,0:T(8,128)S(1)} %tie.2.order_ref.refs_0_), channel_id=1, source_target_pairs={{0,4},{4,0},{8,12},{12,8},{1,5},{5,1},{9,13},{13,9},{2,6},{6,2},{1... | collective-permute-start | bytes 36872 | tf_op jit(solution)/shard_map/ppermute | solution.py:391
  23.7 1.6 %collective-permute-start.6 = (bf16[2,128,512]{2,1,0:T(8,128)(2,1)S(1)}, bf16[2,128,512]{2,1,0:T(8,128)(2,1)S(1)}, u32[]{:S(2)}, u32[]{:S(2)}) collective-permute-start(bf16[2,128,512]{2,1,0:T(8,128)(2,1)S(1)} %down_rows.4._), channel_id=1, source_target_pairs={{0,4},{4,0},{8,12},{12,8},{1,5},{5,1},{9,13},{13,9},{2,6},{6,2},{1... | collective-permute-start | bytes 786440 | tf_op jit(solution)/shard_map/ppermute | solution.py:391
  28.0 4.3 %collective-permute-start.7 = (bf16[2,128,1536]{2,1,0:T(8,128)(2,1)S(1)}, bf16[2,128,1536]{2,1,0:T(8,128)(2,1)S(1)}, u32[]{:S(2)}, u32[]{:S(2)}) collective-permute-start(bf16[2,128,1536]{2,1,0:T(8,128)(2,1)S(1)} %down_rows.6._), channel_id=1, source_target_pairs={{0,4},{4,0},{8,12},{12,8},{1,5},{5,1},{9,13},{13,9},{2,6},{6,2},{1... | collective-permute-start | bytes 2359304 | tf_op jit(solution)/shard_map/ppermute | solution.py:391
  28.2 5.8 %collective-permute-start.8 = (bf16[128,512]{1,0:T(8,128)(2,1)S(1)}, bf16[128,512]{1,0:T(8,128)(2,1)S(1)}, u32[]{:S(2)}, u32[]{:S(2)}) collective-permute-start(bf16[128,512]{1,0:T(8,128)(2,1)S(1)} %bitcast.10), channel_id=1, source_target_pairs={{0,8},{4,12},{8,0},{12,4},{1,9},{5,13},{9,1},{13,5},{2,10},{6,14},... | collective-permute-start | bytes 393224 | tf_op jit(solution)/shard_map/ppermute | solution.py:394
  32.6 6.4 %collective-permute-start.9 = (bf16[128,512]{1,0:T(8,128)(2,1)S(1)}, bf16[128,512]{1,0:T(8,128)(2,1)S(1)}, u32[]{:S(2)}, u32[]{:S(2)}) collective-permute-start(bf16[128,512]{1,0:T(8,128)(2,1)S(1)} %bitcast.11), channel_id=1, source_target_pairs={{0,8},{4,12},{8,0},{12,4},{1,9},{5,13},{9,1},{13,5},{2,10},{6,14},... | collective-permute-start | bytes 393224 | tf_op jit(solution)/shard_map/ppermute | solution.py:394
  34.0 5.0 %collective-permute-start.10 = (bf16[128,512]{1,0:T(8,128)(2,1)S(1)}, bf16[128,512]{1,0:T(8,128)(2,1)S(1)}, u32[]{:S(2)}, u32[]{:S(2)}) collective-permute-start(bf16[128,512]{1,0:T(8,128)(2,1)S(1)} %get-tuple-element.62._), channel_id=1, source_target_pairs={{0,1},{1,0},{2,6},{3,7},{4,5},{5,4},{6,2},{7,3},{8,9},{9,8},{10,14... | collective-permute-start | bytes 393224 | tf_op jit(solution)/shard_map/ppermute | solution.py:378
  34.0 7.0 %collective-permute-start.11 = (bf16[128,512]{1,0:T(8,128)(2,1)S(1)}, bf16[128,512]{1,0:T(8,128)(2,1)S(1)}, u32[]{:S(2)}, u32[]{:S(2)}) collective-permute-start(bf16[128,512]{1,0:T(8,128)(2,1)S(1)} %bitcast.9), channel_id=1, source_target_pairs={{0,8},{4,12},{8,0},{12,4},{1,9},{5,13},{9,1},{13,5},{2,10},{6,14},... | collective-permute-start | bytes 393224 | tf_op jit(solution)/shard_map/ppermute | solution.py:394
  39.1 1.9 %collective-permute-start.12 = (bf16[128,512]{1,0:T(8,128)(2,1)S(1)}, bf16[128,512]{1,0:T(8,128)(2,1)S(1)}, u32[]{:S(2)}, u32[]{:S(2)}) collective-permute-start(bf16[128,512]{1,0:T(8,128)(2,1)S(1)} %get-tuple-element.65._), channel_id=1, source_target_pairs={{0,1},{1,0},{2,6},{3,7},{4,5},{5,4},{6,2},{7,3},{8,9},{9,8},{10,14... | collective-permute-start | bytes 393224 | tf_op jit(solution)/shard_map/ppermute | solution.py:378
  39.1 6.1 %collective-permute-start.13 = (bf16[128,512]{1,0:T(8,128)(2,1)S(1)}, bf16[128,512]{1,0:T(8,128)(2,1)S(1)}, u32[]{:S(2)}, u32[]{:S(2)}) collective-permute-start(bf16[128,512]{1,0:T(8,128)(2,1)S(1)} %bitcast.8), channel_id=1, source_target_pairs={{0,8},{4,12},{8,0},{12,4},{1,9},{5,13},{9,1},{13,5},{2,10},{6,14},... | collective-permute-start | bytes 393224 | tf_op jit(solution)/shard_map/ppermute | solution.py:394
  39.1 6.4 %collective-permute-start.14 = (bf16[128,512]{1,0:T(8,128)(2,1)S(1)}, bf16[128,512]{1,0:T(8,128)(2,1)S(1)}, u32[]{:S(2)}, u32[]{:S(2)}) collective-permute-start(bf16[128,512]{1,0:T(8,128)(2,1)S(1)} %get-tuple-element.67._), channel_id=1, source_target_pairs={{0,4},{1,2},{2,1},{3,7},{4,0},{5,6},{6,5},{7,3},{8,12},{9,10},{10,... | collective-permute-start | bytes 393224 | tf_op jit(solution)/shard_map/ppermute | solution.py:378
  41.0 5.6 %collective-permute-start.15 = (bf16[128,512]{1,0:T(8,128)(2,1)S(1)}, bf16[128,512]{1,0:T(8,128)(2,1)S(1)}, u32[]{:S(2)}, u32[]{:S(2)}) collective-permute-start(bf16[128,512]{1,0:T(8,128)(2,1)S(1)} %get-tuple-element.71._), channel_id=1, source_target_pairs={{0,1},{1,0},{2,6},{3,7},{4,5},{5,4},{6,2},{7,3},{8,9},{9,8},{10,14... | collective-permute-start | bytes 393224 | tf_op jit(solution)/shard_map/ppermute | solution.py:378
  41.0 7.4 %collective-permute-start.16 = (bf16[128,512]{1,0:T(8,128)(2,1)S(1)}, bf16[128,512]{1,0:T(8,128)(2,1)S(1)}, u32[]{:S(2)}, u32[]{:S(2)}) collective-permute-start(bf16[128,512]{1,0:T(8,128)(2,1)S(1)} %get-tuple-element.73._), channel_id=1, source_target_pairs={{0,4},{1,2},{2,1},{3,7},{4,0},{5,6},{6,5},{7,3},{8,12},{9,10},{10,... | collective-permute-start | bytes 393224 | tf_op jit(solution)/shard_map/ppermute | solution.py:378
  45.2 3.4 %collective-permute-start.17 = (bf16[128,512]{1,0:T(8,128)(2,1)S(1)}, bf16[128,512]{1,0:T(8,128)(2,1)S(1)}, u32[]{:S(2)}, u32[]{:S(2)}) collective-permute-start(bf16[128,512]{1,0:T(8,128)(2,1)S(1)} %get-tuple-element.77._), channel_id=1, source_target_pairs={{0,1},{1,0},{2,6},{3,7},{4,5},{5,4},{6,2},{7,3},{8,9},{9,8},{10,14... | collective-permute-start | bytes 393224 | tf_op jit(solution)/shard_map/ppermute | solution.py:378
  45.5 6.4 %collective-permute-start.19 = (bf16[128,512]{1,0:T(8,128)(2,1)S(1)}, bf16[128,512]{1,0:T(8,128)(2,1)S(1)}, u32[]{:S(2)}, u32[]{:S(2)}) collective-permute-start(bf16[128,512]{1,0:T(8,128)(2,1)S(1)} %get-tuple-element.79._), channel_id=1, source_target_pairs={{0,4},{1,5},{2,3},{3,2},{4,0},{5,1},{6,7},{7,6},{8,12},{9,13},{10,... | collective-permute-start | bytes 393224 | tf_op jit(solution)/shard_map/ppermute | solution.py:378
  46.6 5.8 %collective-permute-start.18 = (bf16[128,512]{1,0:T(8,128)(2,1)S(1)}, bf16[128,512]{1,0:T(8,128)(2,1)S(1)}, u32[]{:S(2)}, u32[]{:S(2)}) collective-permute-start(bf16[128,512]{1,0:T(8,128)(2,1)S(1)} %get-tuple-element.81._), channel_id=1, source_target_pairs={{0,4},{1,2},{2,1},{3,7},{4,0},{5,6},{6,5},{7,3},{8,12},{9,10},{10,... | collective-permute-start | bytes 393224 | tf_op jit(solution)/shard_map/ppermute | solution.py:378
  48.5 5.5 %collective-permute-start.21 = (bf16[128,512]{1,0:T(8,128)(2,1)S(1)}, bf16[128,512]{1,0:T(8,128)(2,1)S(1)}, u32[]{:S(2)}, u32[]{:S(2)}) collective-permute-start(bf16[128,512]{1,0:T(8,128)(2,1)S(1)} %get-tuple-element.83._), channel_id=1, source_target_pairs={{0,4},{1,5},{2,3},{3,2},{4,0},{5,1},{6,7},{7,6},{8,12},{9,13},{10,... | collective-permute-start | bytes 393224 | tf_op jit(solution)/shard_map/ppermute | solution.py:378
  48.6 6.4 %collective-permute-start.20 = (bf16[128,512]{1,0:T(8,128)(2,1)S(1)}, bf16[128,512]{1,0:T(8,128)(2,1)S(1)}, u32[]{:S(2)}, u32[]{:S(2)}) collective-permute-start(bf16[128,512]{1,0:T(8,128)(2,1)S(1)} %get-tuple-element.85._), channel_id=1, source_target_pairs={{0,4},{1,2},{2,1},{3,7},{4,0},{5,6},{6,5},{7,3},{8,12},{9,10},{10,... | collective-permute-start | bytes 393224 | tf_op jit(solution)/shard_map/ppermute | solution.py:378
  52.5 5.0 %collective-permute-start.23 = (bf16[128,512]{1,0:T(8,128)(2,1)S(1)}, bf16[128,512]{1,0:T(8,128)(2,1)S(1)}, u32[]{:S(2)}, u32[]{:S(2)}) collective-permute-start(bf16[128,512]{1,0:T(8,128)(2,1)S(1)} %get-tuple-element.87._), channel_id=1, source_target_pairs={{0,4},{1,5},{2,3},{3,2},{4,0},{5,1},{6,7},{7,6},{8,12},{9,13},{10,... | collective-permute-start | bytes 393224 | tf_op jit(solution)/shard_map/ppermute | solution.py:378
  55.1 5.4 %collective-permute-start.22 = (bf16[128,512]{1,0:T(8,128)(2,1)S(1)}, bf16[128,512]{1,0:T(8,128)(2,1)S(1)}, u32[]{:S(2)}, u32[]{:S(2)}) collective-permute-start(bf16[128,512]{1,0:T(8,128)(2,1)S(1)} %get-tuple-element.89._), channel_id=1, source_target_pairs={{0,4},{1,5},{2,3},{3,2},{4,0},{5,1},{6,7},{7,6},{8,12},{9,13},{10,... | collective-permute-start | bytes 393224 | tf_op jit(solution)/shard_map/ppermute | solution.py:378
where the time goes:
time: 61.8 us; the launch traced here: 61.6 us
  Pallas kernels  26.3 us (43%)
  starting transfers between devices  18.2 us (29%)
  waiting for transfers between devices  16.1 us (26%)
  between operations  0.98 us (2%)
    ppermute x12, starting transfers between devices, exchange(): return lax.ppermute(value, ('expert', 'tm'), pairs)  11.4 us
    pallas_call x1, Pallas kernels, near_hidden(): pl.pallas_call(functools.partial(near_kernel, capacity), out_shape=(pltpu...  10.2 us
    ppermute x12, waiting for transfers between devices, exchange(): return lax.ppermute(value, ('expert', 'tm'), pairs)  8.67 us
    pallas_call x4, Pallas kernels, down_rows(): pl.pallas_call(functools.partial(down_kernel, int(send), start), out_shap...  7.3 us
    ppermute x6, waiting for transfers between devices, shifted(): lax.ppermute(value, 'expert', [(i, (i + 2 * by) % members) for i in range...  5.8 us
    ppermute x6, starting transfers between devices, shifted(): lax.ppermute(value, 'expert', [(i, (i + 2 * by) % members) for i in range...  5.66 us
    pallas_call x1, Pallas kernels, far_hidden(): pl.pallas_call(functools.partial(far_kernel, len(tokens)), out_shape=(plt...  5.44 us
    ppermute x6, waiting for transfers between devices, swapped(): return lax.ppermute(value, 'expert', [(i, i ^ 1) for i in range(members)])  1.65 us
  transfers between devices with their start and end apart: 24, of which 14 were waited for; matrix products, arithmetic and copies ran while one was open for 0% of the time, Pallas kernels for 26%

commit v1 on v0

--- a/solution.py
+++ b/solution.py
@@ -331,23 +331,62 @@
     )(*inputs)
 
 
-def write_kernel(result, out, sem):
-    copy = pltpu.make_async_copy(result, out, sem)
-    copy.start()
-    copy.wait()
-
-
-def write_out(result):
-    return pl.pallas_call(
-        write_kernel,
-        out_shape=pltpu.HBM(result.shape, result.dtype),
-        in_specs=[VMEM],
+def write_kernel(first, result, _, out, mark, sems):
+    mark[...] = jnp.zeros_like(mark)
+    last = lax.axis_index("tm") == lax.axis_size("tm") - 1
+    head, tail = pl.ds(0, first), pl.ds(first, result.shape[1] - first)
+    copies = [pltpu.make_async_copy(result.at[:, part], out.at[:, part], sems.at[i]) for i, part in enumerate((head, tail))]
+    copies[0].start()
+
+    @pl.when(jnp.logical_not(last))
+    def _():
+        copies[1].start()
+        copies[1].wait()
+
+    copies[0].wait()
+
+
+def write_most(result, first, order):
+    return pl.pallas_call(
+        functools.partial(write_kernel, first),
+        out_shape=(pltpu.HBM(result.shape, result.dtype), pltpu.VMEM((8, 128), jnp.float32)),
+        in_specs=[VMEM, ANY],
+        out_specs=(HBM, VMEM),
+        scratch_shapes=[pltpu.SemaphoreType.DMA((2,))],
+        compiler_params=SMALL,
+        cost_estimate=BRIEF,
+        name="write_most",
+    )(result, order)
+
+
+def last_kernel(first, backs, start, _, own, *refs):
+    out, block, sem = refs[-3:]
+
+    @pl.when(lax.axis_index("tm") == lax.axis_size("tm") - 1)
+    def _():
+        columns = pl.ds(first, own.shape[1])
+        total = start[:, columns] + own[...]
+        for ref in refs[: backs + 1]:
+            total = total + ref[...].astype(jnp.float32)
+        block[...] = total
+        copy = pltpu.make_async_copy(block, out.at[:, columns], sem)
+        copy.start()
+        copy.wait()
+
+
+def last_step(own, backs, got, first, start, out, order):
+    inputs = [start, order, own, *backs, got, out]
+    return pl.pallas_call(
+        functools.partial(last_kernel, first, len(backs)),
+        out_shape=pltpu.HBM(out.shape, out.dtype),
+        in_specs=[VMEM, ANY] + [VMEM] * (len(inputs) - 3) + [HBM],
         out_specs=HBM,
-        scratch_shapes=[pltpu.SemaphoreType.DMA],
-        compiler_params=SMALL,
-        cost_estimate=BRIEF,
-        name="write_out",
-    )(result)
+        scratch_shapes=[pltpu.VMEM(own.shape, jnp.float32), pltpu.SemaphoreType.DMA],
+        input_output_aliases={len(inputs) - 1: 0},
+        compiler_params=SMALL,
+        cost_estimate=BRIEF,
+        name="last_step",
+    )(*inputs)
 
 
 def tie_kernel(value_ref, order_ref, out_ref):
@@ -439,6 +478,10 @@
                 backs[first + i] = [shifted(sums[2 * i + 1][by - 1], -by) for by in range(1, chips)]
             order = sums[0]
         else:
+            if c == parts - 1 and hop == steps - 1:
+                out, order = write_most(result, c * width, order)
+                out = last_step(owns[c], backs[c], arrived[c], c * width, start, out, order)
+                continue
             send = hop < steps - 1
             *sent, result = chain_step(
                 hop, owns[c], backs[c], arrived.get(c), c * width, send, start, result, order
@@ -446,7 +489,7 @@
             if send:
                 order = sent[0]
                 arrived[c] = exchange(sent[0], hop, members, steps)
-    return write_out(result)[None]
+    return out[None]
 
 
 def solution(mesh):

time: 61.8 us -> 60.8 us (0.984)
  waiting for transfers between devices: 16.1 us -> 15.1 us
    ppermute x12, waiting for transfers between devices: 8.67 us -> 7.69 us  [exchange(): return lax.ppermute(value, ('expert', 'tm'), pairs)]
  transfers between devices with their start and end apart: 24 -> 24, of which waited for: 14 -> 14; matrix products, arithmetic and copies ran while one was open for 0% -> 0% of each run, Pallas kernels for 26% -> 28%
where the time goes in v1:
time: 60.8 us; the launch traced here: 60.6 us
  Pallas kernels  26.3 us (43%)
  starting transfers between devices  18.2 us (30%)
  waiting for transfers between devices  15.1 us (25%)
  between operations  0.99 us (2%)
    ppermute x12, starting transfers between devices, exchange(): return lax.ppermute(value, ('expert', 'tm'), pairs)  11.4 us
    pallas_call x1, Pallas kernels, near_hidden(): pl.pallas_call(functools.partial(near_kernel, capacity), out_shape=(pltpu...  10.2 us
    ppermute x12, waiting for transfers between devices, exchange(): return lax.ppermute(value, ('expert', 'tm'), pairs)  7.69 us
    pallas_call x4, Pallas kernels, down_rows(): pl.pallas_call(functools.partial(down_kernel, int(send), start), out_shap...  7.3 us
    ppermute x6, waiting for transfers between devices, shifted(): lax.ppermute(value, 'expert', [(i, (i + 2 * by) % members) for i in range...  5.8 us
    ppermute x6, starting transfers between devices, shifted(): lax.ppermute(value, 'expert', [(i, (i + 2 * by) % members) for i in range...  5.66 us
    pallas_call x1, Pallas kernels, far_hidden(): pl.pallas_call(functools.partial(far_kernel, len(tokens)), out_shape=(plt...  5.44 us
    ppermute x6, waiting for transfers between devices, swapped(): return lax.ppermute(value, 'expert', [(i, i ^ 1) for i in range(members)])  1.65 us
  transfers between devices with their start and end apart: 24, of which 14 were waited for; matrix products, arithmetic and copies ran while one was open for 0% of the time, Pallas kernels for 28%

profile of v1, /device:TPU:16, one launch (start us, length us, event | category | flops | bytes accessed | tf_op | source)
XLA Modules:
  0.0 60.6 jit_solution(1482904044694608495)
XLA Ops:
  0.0 0.0 collective-permute-start.3
  0.0 1.5 %collective-permute-start = (bf16[128,2048]{1,0:T(8,128)(2,1)}, bf16[128,2048]{1,0:T(8,128)(2,1)S(1)}, u32[]{:S(2)}, u32[]{:S(2)}) collective-permute-start(bf16[128,2048]{1,0:T(8,128)(2,1)} %bitcast.13), channel_id=1, source_target_pairs={{0,8},{4,12},{8,0},{12,4},{1,9},{5,13},{9,1},{13,5},{2,10},{6,14},... | collective-permute-start | bytes 1572872 | tf_op jit(solution)/shard_map/ppermute | solution.py:433
  1.5 1.3 %make_table.1 = (f32[24,128]{1,0:T(8,128)S(1)}, bf16[128,2048]{1,0:T(8,128)(2,1)S(1)}) custom-call(s32[6,1,128]{2,1,0:T(1,128)} %bitcast.14, f32[6,1,128]{2,1,0:T(1,128)} %bitcast.15, bf16[1,128,2048]{2,1,0:T(8,128)(2,1)} %tokens_hbm.1), custom_call_target="tpu_custom_call" | custom-call | tf_op jit(solution)/shard_map/make_table/pallas_call | solution.py:56
  2.9 0.3 collective-permute-start.2
  3.2 0.5 collective-permute-start.1
  3.7 0.4 collective-permute-done.2.refs_1_
  4.1 10.2 %near_hidden.1 = (bf16[512,3072]{1,0:T(8,128)(2,1)S(1)}, bf16[4,2048,768]{2,1,0:T(8,128)(2,1)S(1)}, bf16[4,2048,768]{2,1,0:T(8,128)(2,1)S(1)}) custom-call(f32[24,128]{1,0:T(8,128)S(1)} %get-tuple-element.50.refs_0_, f32[24,128]{1,0:T(8,128)S(1)} %collective-permute-done.2.refs_1_, bf16[128,2048]{1,0:T(8,128)(2,1)S(1)} %get-tuple-element.51.refs_2_, ...), custom_call_target="tpu_custom_call" | custom-call | flops 3623878656 | bytes 25165824 | tf_op jit(solution)/shard_map/near_hidden/pallas_call | solution.py:146
  14.3 0.5 collective-permute-done.1.value_ref
  14.8 0.0 collective-permute-done.value_ref
  14.8 0.5 collective-permute-start.5
  16.0 0.8 %collective-permute-done.5.refs_1_ = f32[24,128]{1,0:T(8,128)S(1)} collective-permute-done((f32[24,128]{1,0:T(8,128)S(1)}, f32[24,128]{1,0:T(8,128)S(1)}, u32[]{:S(2)}, u32[]{:S(2)}) %collective-permute-start.5) | collective-permute-done | bytes 12320 | tf_op jit(solution)/shard_map/ppermute | solution.py:430
  16.7 0.4 far_plan.1
  17.1 5.4 %far_hidden.1 = (bf16[512,3072]{1,0:T(8,128)(2,1)S(1)}, bf16[4,768,2048]{2,1,0:T(8,128)(2,1)S(1)}, f32[128,2048]{1,0:T(8,128)S(1)}) custom-call(bf16[128,2048]{1,0:T(8,128)(2,1)S(1)} %tie.3.refs_0_, bf16[128,2048]{1,0:T(8,128)(2,1)S(1)} %collective-permute-done.4.refs_1_, ...), custom_call_target="tpu_custom_call", output_to_operand_aliasing={{0}: (8, {})} | custom-call | flops 3623878656 | bytes 37748736 | tf_op jit(solution)/shard_map/far_hidden/pallas_call | solution.py:220
  22.6 1.2 %down_rows.4._ = bf16[2,128,512]{2,1,0:T(8,128)(2,1)S(1)} custom-call(bf16[512,3072]{1,0:T(8,128)(2,1)S(1)} %get-tuple-element.58.hidden_ref._, bf16[4,768,2048]{2,1,0:T(8,128)(2,1)S(1)} %get-tuple-element.59.down_ref, bf16[512,3072]{1,0:T(8,128)(2,1)S(1)} %get-tuple-element.58.hidden_ref._), custom_call_target="tpu_custom_call" | custom-call | tf_op jit(solution)/shard_map/down_rows/pallas_call | solution.py:262
  23.7 0.2 collective-permute-start.6
  23.9 1.0 %down_rows.5.keep._ = f32[2,128,512]{2,1,0:T(8,128)S(1)} custom-call(bf16[512,3072]{1,0:T(8,128)(2,1)S(1)} %get-tuple-element.58.hidden_ref._, bf16[4,768,2048]{2,1,0:T(8,128)(2,1)S(1)} %get-tuple-element.59.down_ref, bf16[2,128,512]{2,1,0:T(8,128)(2,1)S(1)} %down_rows.4._), custom_call_target="tpu_custom_call" | custom-call | tf_op jit(solution)/shard_map/down_rows/pallas_call | solution.py:262
  24.9 0.4 collective-permute-done.6.got
  25.3 0.1 core_sum.2
  25.4 2.6 %down_rows.6._ = bf16[2,128,1536]{2,1,0:T(8,128)(2,1)S(1)} custom-call(bf16[512,3072]{1,0:T(8,128)(2,1)S(1)} %get-tuple-element.58.hidden_ref._, bf16[4,768,2048]{2,1,0:T(8,128)(2,1)S(1)} %get-tuple-element.59.down_ref, f32[128,512]{1,0:T(8,128)S(1)} %get-tuple-element.61._.own), custom_call_target="tpu_custom_call" | custom-call | tf_op jit(solution)/shard_map/down_rows/pallas_call | solution.py:262
  28.0 0.2 collective-permute-start.7
  28.2 1.5 %collective-permute-start.8 = (bf16[128,512]{1,0:T(8,128)(2,1)S(1)}, bf16[128,512]{1,0:T(8,128)(2,1)S(1)}, u32[]{:S(2)}, u32[]{:S(2)}) collective-permute-start(bf16[128,512]{1,0:T(8,128)(2,1)S(1)} %bitcast.10), channel_id=1, source_target_pairs={{0,8},{4,12},{8,0},{12,4},{1,9},{5,13},{9,1},{13,5},{2,10},{6,14},... | collective-permute-start | bytes 393224 | tf_op jit(solution)/shard_map/ppermute | solution.py:433
  29.8 2.6 %down_rows.7.keep._ = f32[2,128,1536]{2,1,0:T(8,128)S(1)} custom-call(bf16[512,3072]{1,0:T(8,128)(2,1)S(1)} %get-tuple-element.58.hidden_ref._, bf16[4,768,2048]{2,1,0:T(8,128)(2,1)S(1)} %get-tuple-element.59.down_ref, bf16[2,128,1536]{2,1,0:T(8,128)(2,1)S(1)} %down_rows.6._), custom_call_target="tpu_custom_call" | custom-call | tf_op jit(solution)/shard_map/down_rows/pallas_call | solution.py:262
  32.4 0.2 core_sum.3
  32.6 0.6 collective-permute-start.9
  33.2 0.8 %collective-permute-done.8.refs_0_ = bf16[128,512]{1,0:T(8,128)(2,1)S(1)} collective-permute-done((bf16[128,512]{1,0:T(8,128)(2,1)S(1)}, bf16[128,512]{1,0:T(8,128)(2,1)S(1)}, u32[]{:S(2)}, u32[]{:S(2)}) %collective-permute-start.8) | collective-permute-done | bytes 131104 | tf_op jit(solution)/shard_map/ppermute | solution.py:433
  34.0 1.5 %collective-permute-start.11 = (bf16[128,512]{1,0:T(8,128)(2,1)S(1)}, bf16[128,512]{1,0:T(8,128)(2,1)S(1)}, u32[]{:S(2)}, u32[]{:S(2)}) collective-permute-start(bf16[128,512]{1,0:T(8,128)(2,1)S(1)} %bitcast.9), channel_id=1, source_target_pairs={{0,8},{4,12},{8,0},{12,4},{1,9},{5,13},{9,1},{13,5},{2,10},{6,14},... | collective-permute-start | bytes 393224 | tf_op jit(solution)/shard_map/ppermute | solution.py:433
  35.5 3.5 %collective-permute-done.9.refs_0_ = bf16[128,512]{1,0:T(8,128)(2,1)S(1)} collective-permute-done((bf16[128,512]{1,0:T(8,128)(2,1)S(1)}, bf16[128,512]{1,0:T(8,128)(2,1)S(1)}, u32[]{:S(2)}, u32[]{:S(2)}) %collective-permute-start.9) | collective-permute-done | bytes 131104 | tf_op jit(solution)/shard_map/ppermute | solution.py:433
  39.1 0.9 %collective-permute-start.14 = (bf16[128,512]{1,0:T(8,128)(2,1)S(1)}, bf16[128,512]{1,0:T(8,128)(2,1)S(1)}, u32[]{:S(2)}, u32[]{:S(2)}) collective-permute-start(bf16[128,512]{1,0:T(8,128)(2,1)S(1)} %get-tuple-element.69._), channel_id=1, source_target_pairs={{0,4},{1,2},{2,1},{3,7},{4,0},{5,6},{6,5},{7,3},{8,12},{9,10},{10,... | collective-permute-start | bytes 393224 | tf_op jit(solution)/shard_map/ppermute | solution.py:417
  40.0 1.0 %collective-permute-done.11.refs_0_ = bf16[128,512]{1,0:T(8,128)(2,1)S(1)} collective-permute-done((bf16[128,512]{1,0:T(8,128)(2,1)S(1)}, bf16[128,512]{1,0:T(8,128)(2,1)S(1)}, u32[]{:S(2)}, u32[]{:S(2)}) %collective-permute-start.11) | collective-permute-done | bytes 131104 | tf_op jit(solution)/shard_map/ppermute | solution.py:433
  41.0 4.2 %collective-permute-start.16 = (bf16[128,512]{1,0:T(8,128)(2,1)S(1)}, bf16[128,512]{1,0:T(8,128)(2,1)S(1)}, u32[]{:S(2)}, u32[]{:S(2)}) collective-permute-start(bf16[128,512]{1,0:T(8,128)(2,1)S(1)} %get-tuple-element.75._), channel_id=1, source_target_pairs={{0,4},{1,2},{2,1},{3,7},{4,0},{5,6},{6,5},{7,3},{8,12},{9,10},{10,... | collective-permute-start | bytes 393224 | tf_op jit(solution)/shard_map/ppermute | solution.py:417
  45.2 0.3 collective-permute-done.14.refs_1_
  45.5 0.1 chain_step.21
  45.5 1.1 %collective-permute-start.19 = (bf16[128,512]{1,0:T(8,128)(2,1)S(1)}, bf16[128,512]{1,0:T(8,128)(2,1)S(1)}, u32[]{:S(2)}, u32[]{:S(2)}) collective-permute-start(bf16[128,512]{1,0:T(8,128)(2,1)S(1)} %get-tuple-element.81._), channel_id=1, source_target_pairs={{0,4},{1,5},{2,3},{3,2},{4,0},{5,1},{6,7},{7,6},{8,12},{9,13},{10,... | collective-permute-start | bytes 393224 | tf_op jit(solution)/shard_map/ppermute | solution.py:417
  46.6 1.8 %collective-permute-start.18 = (bf16[128,512]{1,0:T(8,128)(2,1)S(1)}, bf16[128,512]{1,0:T(8,128)(2,1)S(1)}, u32[]{:S(2)}, u32[]{:S(2)}) collective-permute-start(bf16[128,512]{1,0:T(8,128)(2,1)S(1)} %get-tuple-element.83._), channel_id=1, source_target_pairs={{0,4},{1,2},{2,1},{3,7},{4,0},{5,6},{6,5},{7,3},{8,12},{9,10},{10,... | collective-permute-start | bytes 393224 | tf_op jit(solution)/shard_map/ppermute | solution.py:417
  48.4 0.1 chain_step.23
  48.5 0.1 collective-permute-start.21
  48.6 2.0 %collective-permute-start.20 = (bf16[128,512]{1,0:T(8,128)(2,1)S(1)}, bf16[128,512]{1,0:T(8,128)(2,1)S(1)}, u32[]{:S(2)}, u32[]{:S(2)}) collective-permute-start(bf16[128,512]{1,0:T(8,128)(2,1)S(1)} %get-tuple-element.87._), channel_id=1, source_target_pairs={{0,4},{1,2},{2,1},{3,7},{4,0},{5,6},{6,5},{7,3},{8,12},{9,10},{10,... | collective-permute-start | bytes 393224 | tf_op jit(solution)/shard_map/ppermute | solution.py:417
  50.6 1.3 %collective-permute-done.19.refs_1_ = bf16[128,512]{1,0:T(8,128)(2,1)S(1)} collective-permute-done((bf16[128,512]{1,0:T(8,128)(2,1)S(1)}, bf16[128,512]{1,0:T(8,128)(2,1)S(1)}, u32[]{:S(2)}, u32[]{:S(2)}) %collective-permute-start.19) | collective-permute-done | bytes 131104 | tf_op jit(solution)/shard_map/ppermute | solution.py:417
  51.9 0.5 collective-permute-done.18.refs_1_
  52.4 0.1 chain_step.26
  52.5 0.6 %collective-permute-start.22 = (bf16[128,512]{1,0:T(8,128)(2,1)S(1)}, bf16[128,512]{1,0:T(8,128)(2,1)S(1)}, u32[]{:S(2)}, u32[]{:S(2)}) collective-permute-start(bf16[128,512]{1,0:T(8,128)(2,1)S(1)} %get-tuple-element.89._), channel_id=1, source_target_pairs={{0,4},{1,5},{2,3},{3,2},{4,0},{5,1},{6,7},{7,6},{8,12},{9,13},{10,... | collective-permute-start | bytes 393224 | tf_op jit(solution)/shard_map/ppermute | solution.py:417
  53.1 1.0 %collective-permute-done.21.refs_1_ = bf16[128,512]{1,0:T(8,128)(2,1)S(1)} collective-permute-done((bf16[128,512]{1,0:T(8,128)(2,1)S(1)}, bf16[128,512]{1,0:T(8,128)(2,1)S(1)}, u32[]{:S(2)}, u32[]{:S(2)}) %collective-permute-start.21) | collective-permute-done | bytes 131104 | tf_op jit(solution)/shard_map/ppermute | solution.py:417
  54.0 1.0 %collective-permute-done.20.refs_1_ = bf16[128,512]{1,0:T(8,128)(2,1)S(1)} collective-permute-done((bf16[128,512]{1,0:T(8,128)(2,1)S(1)}, bf16[128,512]{1,0:T(8,128)(2,1)S(1)}, u32[]{:S(2)}, u32[]{:S(2)}) %collective-permute-start.20) | collective-permute-done | bytes 131104 | tf_op jit(solution)/shard_map/ppermute | solution.py:417
  55.0 0.1 chain_step.28
  55.1 0.7 %collective-permute-start.23 = (bf16[128,512]{1,0:T(8,128)(2,1)S(1)}, bf16[128,512]{1,0:T(8,128)(2,1)S(1)}, u32[]{:S(2)}, u32[]{:S(2)}) collective-permute-start(bf16[128,512]{1,0:T(8,128)(2,1)S(1)} %get-tuple-element.91._), channel_id=1, source_target_pairs={{0,4},{1,5},{2,3},{3,2},{4,0},{5,1},{6,7},{7,6},{8,12},{9,13},{10,... | collective-permute-start | bytes 393224 | tf_op jit(solution)/shard_map/ppermute | solution.py:417
  55.8 1.7 %collective-permute-done.22.refs_1_ = bf16[128,512]{1,0:T(8,128)(2,1)S(1)} collective-permute-done((bf16[128,512]{1,0:T(8,128)(2,1)S(1)}, bf16[128,512]{1,0:T(8,128)(2,1)S(1)}, u32[]{:S(2)}, u32[]{:S(2)}) %collective-permute-start.22) | collective-permute-done | bytes 131104 | tf_op jit(solution)/shard_map/ppermute | solution.py:417
  57.5 1.0 %write_most.1 = (f32[128,2048]{1,0:T(8,128)}, f32[8,128]{1,0:T(8,128)S(1)}) custom-call(f32[128,2048]{1,0:T(8,128)S(1)} %chain_step.29.result, bf16[128,512]{1,0:T(8,128)(2,1)S(1)} %get-tuple-element.91._), custom_call_target="tpu_custom_call" | custom-call | tf_op jit(solution)/shard_map/write_most/pallas_call | solution.py:350
  58.5 1.9 %collective-permute-done.23.refs_1_ = bf16[128,512]{1,0:T(8,128)(2,1)S(1)} collective-permute-done((bf16[128,512]{1,0:T(8,128)(2,1)S(1)}, bf16[128,512]{1,0:T(8,128)(2,1)S(1)}, u32[]{:S(2)}, u32[]{:S(2)}) %collective-permute-start.23) | collective-permute-done | bytes 131104 | tf_op jit(solution)/shard_map/ppermute | solution.py:417
  (29 shorter events, 0.1 us)
Async XLA Ops:
  0.0 4.1 %collective-permute-start.3 = (bf16[128,2048]{1,0:T(8,128)(2,1)}, bf16[128,2048]{1,0:T(8,128)(2,1)S(1)}, u32[]{:S(2)}, u32[]{:S(2)}) collective-permute-start(bf16[128,2048]{1,0:T(8,128)(2,1)} %bitcast.12), channel_id=1, source_target_pairs={{0,4},{4,0},{8,12},{12,8},{1,5},{5,1},{9,13},{13,9},{2,6},{6,2},{1... | collective-permute-start | bytes 1572872 | tf_op jit(solution)/shard_map/ppermute | solution.py:430
  0.0 14.8 %collective-permute-start = (bf16[128,2048]{1,0:T(8,128)(2,1)}, bf16[128,2048]{1,0:T(8,128)(2,1)S(1)}, u32[]{:S(2)}, u32[]{:S(2)}) collective-permute-start(bf16[128,2048]{1,0:T(8,128)(2,1)} %bitcast.13), channel_id=1, source_target_pairs={{0,8},{4,12},{8,0},{12,4},{1,9},{5,13},{9,1},{13,5},{2,10},{6,14},... | collective-permute-start | bytes 1572872 | tf_op jit(solution)/shard_map/ppermute | solution.py:433
  2.9 1.2 %collective-permute-start.2 = (f32[24,128]{1,0:T(8,128)S(1)}, f32[24,128]{1,0:T(8,128)S(1)}, u32[]{:S(2)}, u32[]{:S(2)}) collective-permute-start(f32[24,128]{1,0:T(8,128)S(1)} %get-tuple-element.50.refs_0_), channel_id=1, source_target_pairs={{0,4},{4,0},{8,12},{12,8},{1,5},{5,1},{9,13},{13,9},{2,6},{6,2},{1... | collective-permute-start | bytes 36872 | tf_op jit(solution)/shard_map/ppermute | solution.py:430
  3.2 11.7 %collective-permute-start.1 = (f32[24,128]{1,0:T(8,128)S(1)}, f32[24,128]{1,0:T(8,128)S(1)}, u32[]{:S(2)}, u32[]{:S(2)}) collective-permute-start(f32[24,128]{1,0:T(8,128)S(1)} %get-tuple-element.50.refs_0_), channel_id=1, source_target_pairs={{0,8},{4,12},{8,0},{12,4},{1,9},{5,13},{9,1},{13,5},{2,10},{6,14},... | collective-permute-start | bytes 36872 | tf_op jit(solution)/shard_map/ppermute | solution.py:433
  14.8 2.3 %collective-permute-start.4 = (bf16[128,2048]{1,0:T(8,128)(2,1)S(1)}, bf16[128,2048]{1,0:T(8,128)(2,1)S(1)}, u32[]{:S(2)}, u32[]{:S(2)}) collective-permute-start(bf16[128,2048]{1,0:T(8,128)(2,1)S(1)} %tie.3.refs_0_), channel_id=1, source_target_pairs={{0,4},{4,0},{8,12},{12,8},{1,5},{5,1},{9,13},{13,9},{2,6},{6,2},{1... | collective-permute-start | bytes 1572872 | tf_op jit(solution)/shard_map/ppermute | solution.py:430
  14.8 1.9 %collective-permute-start.5 = (f32[24,128]{1,0:T(8,128)S(1)}, f32[24,128]{1,0:T(8,128)S(1)}, u32[]{:S(2)}, u32[]{:S(2)}) collective-permute-start(f32[24,128]{1,0:T(8,128)S(1)} %tie.2.order_ref.refs_0_), channel_id=1, source_target_pairs={{0,4},{4,0},{8,12},{12,8},{1,5},{5,1},{9,13},{13,9},{2,6},{6,2},{1... | collective-permute-start | bytes 36872 | tf_op jit(solution)/shard_map/ppermute | solution.py:430
  23.7 1.6 %collective-permute-start.6 = (bf16[2,128,512]{2,1,0:T(8,128)(2,1)S(1)}, bf16[2,128,512]{2,1,0:T(8,128)(2,1)S(1)}, u32[]{:S(2)}, u32[]{:S(2)}) collective-permute-start(bf16[2,128,512]{2,1,0:T(8,128)(2,1)S(1)} %down_rows.4._), channel_id=1, source_target_pairs={{0,4},{4,0},{8,12},{12,8},{1,5},{5,1},{9,13},{13,9},{2,6},{6,2},{1... | collective-permute-start | bytes 786440 | tf_op jit(solution)/shard_map/ppermute | solution.py:430
  28.0 4.3 %collective-permute-start.7 = (bf16[2,128,1536]{2,1,0:T(8,128)(2,1)S(1)}, bf16[2,128,1536]{2,1,0:T(8,128)(2,1)S(1)}, u32[]{:S(2)}, u32[]{:S(2)}) collective-permute-start(bf16[2,128,1536]{2,1,0:T(8,128)(2,1)S(1)} %down_rows.6._), channel_id=1, source_target_pairs={{0,4},{4,0},{8,12},{12,8},{1,5},{5,1},{9,13},{13,9},{2,6},{6,2},{1... | collective-permute-start | bytes 2359304 | tf_op jit(solution)/shard_map/ppermute | solution.py:430
  28.2 5.8 %collective-permute-start.8 = (bf16[128,512]{1,0:T(8,128)(2,1)S(1)}, bf16[128,512]{1,0:T(8,128)(2,1)S(1)}, u32[]{:S(2)}, u32[]{:S(2)}) collective-permute-start(bf16[128,512]{1,0:T(8,128)(2,1)S(1)} %bitcast.10), channel_id=1, source_target_pairs={{0,8},{4,12},{8,0},{12,4},{1,9},{5,13},{9,1},{13,5},{2,10},{6,14},... | collective-permute-start | bytes 393224 | tf_op jit(solution)/shard_map/ppermute | solution.py:433
  32.6 6.4 %collective-permute-start.9 = (bf16[128,512]{1,0:T(8,128)(2,1)S(1)}, bf16[128,512]{1,0:T(8,128)(2,1)S(1)}, u32[]{:S(2)}, u32[]{:S(2)}) collective-permute-start(bf16[128,512]{1,0:T(8,128)(2,1)S(1)} %bitcast.11), channel_id=1, source_target_pairs={{0,8},{4,12},{8,0},{12,4},{1,9},{5,13},{9,1},{13,5},{2,10},{6,14},... | collective-permute-start | bytes 393224 | tf_op jit(solution)/shard_map/ppermute | solution.py:433
  34.0 5.0 %collective-permute-start.10 = (bf16[128,512]{1,0:T(8,128)(2,1)S(1)}, bf16[128,512]{1,0:T(8,128)(2,1)S(1)}, u32[]{:S(2)}, u32[]{:S(2)}) collective-permute-start(bf16[128,512]{1,0:T(8,128)(2,1)S(1)} %get-tuple-element.64._), channel_id=1, source_target_pairs={{0,1},{1,0},{2,6},{3,7},{4,5},{5,4},{6,2},{7,3},{8,9},{9,8},{10,14... | collective-permute-start | bytes 393224 | tf_op jit(solution)/shard_map/ppermute | solution.py:417
  34.0 7.0 %collective-permute-start.11 = (bf16[128,512]{1,0:T(8,128)(2,1)S(1)}, bf16[128,512]{1,0:T(8,128)(2,1)S(1)}, u32[]{:S(2)}, u32[]{:S(2)}) collective-permute-start(bf16[128,512]{1,0:T(8,128)(2,1)S(1)} %bitcast.9), channel_id=1, source_target_pairs={{0,8},{4,12},{8,0},{12,4},{1,9},{5,13},{9,1},{13,5},{2,10},{6,14},... | collective-permute-start | bytes 393224 | tf_op jit(solution)/shard_map/ppermute | solution.py:433
  39.1 1.9 %collective-permute-start.12 = (bf16[128,512]{1,0:T(8,128)(2,1)S(1)}, bf16[128,512]{1,0:T(8,128)(2,1)S(1)}, u32[]{:S(2)}, u32[]{:S(2)}) collective-permute-start(bf16[128,512]{1,0:T(8,128)(2,1)S(1)} %get-tuple-element.67._), channel_id=1, source_target_pairs={{0,1},{1,0},{2,6},{3,7},{4,5},{5,4},{6,2},{7,3},{8,9},{9,8},{10,14... | collective-permute-start | bytes 393224 | tf_op jit(solution)/shard_map/ppermute | solution.py:417
  39.1 6.1 %collective-permute-start.13 = (bf16[128,512]{1,0:T(8,128)(2,1)S(1)}, bf16[128,512]{1,0:T(8,128)(2,1)S(1)}, u32[]{:S(2)}, u32[]{:S(2)}) collective-permute-start(bf16[128,512]{1,0:T(8,128)(2,1)S(1)} %bitcast.8), channel_id=1, source_target_pairs={{0,8},{4,12},{8,0},{12,4},{1,9},{5,13},{9,1},{13,5},{2,10},{6,14},... | collective-permute-start | bytes 393224 | tf_op jit(solution)/shard_map/ppermute | solution.py:433
  39.1 6.4 %collective-permute-start.14 = (bf16[128,512]{1,0:T(8,128)(2,1)S(1)}, bf16[128,512]{1,0:T(8,128)(2,1)S(1)}, u32[]{:S(2)}, u32[]{:S(2)}) collective-permute-start(bf16[128,512]{1,0:T(8,128)(2,1)S(1)} %get-tuple-element.69._), channel_id=1, source_target_pairs={{0,4},{1,2},{2,1},{3,7},{4,0},{5,6},{6,5},{7,3},{8,12},{9,10},{10,... | collective-permute-start | bytes 393224 | tf_op jit(solution)/shard_map/ppermute | solution.py:417
  41.0 5.6 %collective-permute-start.15 = (bf16[128,512]{1,0:T(8,128)(2,1)S(1)}, bf16[128,512]{1,0:T(8,128)(2,1)S(1)}, u32[]{:S(2)}, u32[]{:S(2)}) collective-permute-start(bf16[128,512]{1,0:T(8,128)(2,1)S(1)} %get-tuple-element.73._), channel_id=1, source_target_pairs={{0,1},{1,0},{2,6},{3,7},{4,5},{5,4},{6,2},{7,3},{8,9},{9,8},{10,14... | collective-permute-start | bytes 393224 | tf_op jit(solution)/shard_map/ppermute | solution.py:417
  41.0 7.4 %collective-permute-start.16 = (bf16[128,512]{1,0:T(8,128)(2,1)S(1)}, bf16[128,512]{1,0:T(8,128)(2,1)S(1)}, u32[]{:S(2)}, u32[]{:S(2)}) collective-permute-start(bf16[128,512]{1,0:T(8,128)(2,1)S(1)} %get-tuple-element.75._), channel_id=1, source_target_pairs={{0,4},{1,2},{2,1},{3,7},{4,0},{5,6},{6,5},{7,3},{8,12},{9,10},{10,... | collective-permute-start | bytes 393224 | tf_op jit(solution)/shard_map/ppermute | solution.py:417
  45.2 3.4 %collective-permute-start.17 = (bf16[128,512]{1,0:T(8,128)(2,1)S(1)}, bf16[128,512]{1,0:T(8,128)(2,1)S(1)}, u32[]{:S(2)}, u32[]{:S(2)}) collective-permute-start(bf16[128,512]{1,0:T(8,128)(2,1)S(1)} %get-tuple-element.79._), channel_id=1, source_target_pairs={{0,1},{1,0},{2,6},{3,7},{4,5},{5,4},{6,2},{7,3},{8,9},{9,8},{10,14... | collective-permute-start | bytes 393224 | tf_op jit(solution)/shard_map/ppermute | solution.py:417
  45.5 6.4 %collective-permute-start.19 = (bf16[128,512]{1,0:T(8,128)(2,1)S(1)}, bf16[128,512]{1,0:T(8,128)(2,1)S(1)}, u32[]{:S(2)}, u32[]{:S(2)}) collective-permute-start(bf16[128,512]{1,0:T(8,128)(2,1)S(1)} %get-tuple-element.81._), channel_id=1, source_target_pairs={{0,4},{1,5},{2,3},{3,2},{4,0},{5,1},{6,7},{7,6},{8,12},{9,13},{10,... | collective-permute-start | bytes 393224 | tf_op jit(solution)/shard_map/ppermute | solution.py:417
  46.6 5.8 %collective-permute-start.18 = (bf16[128,512]{1,0:T(8,128)(2,1)S(1)}, bf16[128,512]{1,0:T(8,128)(2,1)S(1)}, u32[]{:S(2)}, u32[]{:S(2)}) collective-permute-start(bf16[128,512]{1,0:T(8,128)(2,1)S(1)} %get-tuple-element.83._), channel_id=1, source_target_pairs={{0,4},{1,2},{2,1},{3,7},{4,0},{5,6},{6,5},{7,3},{8,12},{9,10},{10,... | collective-permute-start | bytes 393224 | tf_op jit(solution)/shard_map/ppermute | solution.py:417
  48.5 5.5 %collective-permute-start.21 = (bf16[128,512]{1,0:T(8,128)(2,1)S(1)}, bf16[128,512]{1,0:T(8,128)(2,1)S(1)}, u32[]{:S(2)}, u32[]{:S(2)}) collective-permute-start(bf16[128,512]{1,0:T(8,128)(2,1)S(1)} %get-tuple-element.85._), channel_id=1, source_target_pairs={{0,4},{1,5},{2,3},{3,2},{4,0},{5,1},{6,7},{7,6},{8,12},{9,13},{10,... | collective-permute-start | bytes 393224 | tf_op jit(solution)/shard_map/ppermute | solution.py:417
  48.6 6.4 %collective-permute-start.20 = (bf16[128,512]{1,0:T(8,128)(2,1)S(1)}, bf16[128,512]{1,0:T(8,128)(2,1)S(1)}, u32[]{:S(2)}, u32[]{:S(2)}) collective-permute-start(bf16[128,512]{1,0:T(8,128)(2,1)S(1)} %get-tuple-element.87._), channel_id=1, source_target_pairs={{0,4},{1,2},{2,1},{3,7},{4,0},{5,6},{6,5},{7,3},{8,12},{9,10},{10,... | collective-permute-start | bytes 393224 | tf_op jit(solution)/shard_map/ppermute | solution.py:417
  52.5 5.0 %collective-permute-start.22 = (bf16[128,512]{1,0:T(8,128)(2,1)S(1)}, bf16[128,512]{1,0:T(8,128)(2,1)S(1)}, u32[]{:S(2)}, u32[]{:S(2)}) collective-permute-start(bf16[128,512]{1,0:T(8,128)(2,1)S(1)} %get-tuple-element.89._), channel_id=1, source_target_pairs={{0,4},{1,5},{2,3},{3,2},{4,0},{5,1},{6,7},{7,6},{8,12},{9,13},{10,... | collective-permute-start | bytes 393224 | tf_op jit(solution)/shard_map/ppermute | solution.py:417
  55.1 5.4 %collective-permute-start.23 = (bf16[128,512]{1,0:T(8,128)(2,1)S(1)}, bf16[128,512]{1,0:T(8,128)(2,1)S(1)}, u32[]{:S(2)}, u32[]{:S(2)}) collective-permute-start(bf16[128,512]{1,0:T(8,128)(2,1)S(1)} %get-tuple-element.91._), channel_id=1, source_target_pairs={{0,4},{1,5},{2,3},{3,2},{4,0},{5,1},{6,7},{7,6},{8,12},{9,13},{10,... | collective-permute-start | bytes 393224 | tf_op jit(solution)/shard_map/ppermute | solution.py:417
